TPU v7x, 512 devices: a whole 4x8x8 slice. The times are simulated.
512 devices in a mesh: dp: 16 (over x, z_lo, core), ctx: 32 (over z_hi, y).
Axes of the slice: x: 4, y: 8, z: 8 (z_hi: 4, z_lo: 2; z = z_hi * 2 + z_lo), core: 2. Of those that a mesh axis runs over, the one named last changes fastest.
Arguments:
- queries: bfloat16 [16, 4096, 1024], P('dp', 'ctx'), may hold values from -60 to 60
- keys: bfloat16 [16, 4096, 128], P('dp', 'ctx'), may hold values from -6 to 6
- values: bfloat16 [16, 4096, 192], P('dp', 'ctx'), may hold values from -96 to 96
- features_fine: bfloat16 [16, 8192, 1536], P('dp', 'ctx'), may hold values from -6 to 6
- rc_state: bfloat16 [16, 4096, 1536], P('dp', 'ctx'), may hold values from -6 to 6
- conv_weight: float32 [5, 1536], replicated, may hold values from -2.5 to 2.5
Outputs:
- d_fine: bfloat16 [16, 8192, 1536], P('dp', 'ctx')
- d_weight: float32 [5, 1536], replicated
All inputs are finite; a program needn't handle non-finite values.
Results may differ from a plain program's by a relative error of at most 0.0085.
Values may be sent and summed in bfloat16 or wider, within the bound.
A program may use at most 64 MiB of HBM per device.

v0:
```python
import math

import jax
import jax.numpy as jnp
from jax import lax
from jax.sharding import PartitionSpec as P

HEADS = 8
KW = 5


def padded_2(cells, sides, width):
    for axis, dim in sides:
        count = lax.axis_size(axis)
        ends = count - 1
        head = lax.slice_in_dim(cells, 0, width, axis=dim)
        tail = lax.slice_in_dim(cells, cells.shape[dim] - width, cells.shape[dim], axis=dim)
        cells = jnp.concatenate(
            [
                lax.ppermute(tail, axis, [(i, (i + 1) % count) for i in range(ends)]),
                cells,
                lax.ppermute(head, axis, [((i + 1) % count, i) for i in range(ends)]),
            ],
            axis=dim,
        )
    return cells


def body(queries, keys, values, features_fine, rc_state, conv_weight):
    tok_rows = queries.shape[1]
    key_size = keys.shape[2]
    value_size = values.shape[2]
    q_heads = queries[0].reshape(tok_rows, HEADS, key_size)
    ctx_count = lax.axis_size("ctx")
    run_top = jnp.full((tok_rows, HEADS), -1e30, jnp.float32)
    key_piece = lax.all_gather(keys, "ctx", axis=1, tiled=True)
    value_piece = lax.all_gather(values, "ctx", axis=1, tiled=True)
    scores = jnp.einsum(
        "qhd,kd->qhk", q_heads, key_piece[0], preferred_element_type=jnp.float32
    ) * key_size ** (-0.5)
    new_top = jnp.maximum(run_top, jnp.max(scores, axis=-1))
    expd = jnp.exp(scores - new_top[..., None])
    new_total = jnp.sum(expd, axis=-1)
    mixed = jnp.einsum(
        "qhk,kv->qhv", expd.astype(jnp.bfloat16), value_piece[0], preferred_element_type=jnp.float32
    )
    attended = (mixed / new_total[..., None]).reshape(tok_rows, HEADS * value_size)[None]
    padded = padded_2(features_fine, (("ctx", 1),), 2)
    taps = [padded[:, k : k + 2 * tok_rows : 2, :].astype(jnp.float32) for k in range(KW)]
    coarse = conv_weight[0] * taps[0]
    for k in range(1, KW):
        coarse = coarse + conv_weight[k] * taps[k]
    slices = lax.all_to_all(rc_state, "ctx", split_axis=2, concat_axis=0, tiled=True)
    flipped = slices[::-1]
    mirrored = lax.all_to_all(flipped, "ctx", split_axis=0, concat_axis=2, tiled=True)
    grad = coarse + attended - mirrored[:, ::-1, :].astype(jnp.float32)
    gpad = padded_2(grad.astype(jnp.bfloat16), (("ctx", 1),), 1).astype(grad.dtype)
    even = (
        conv_weight[0] * gpad[:, 2:]
        + conv_weight[2] * gpad[:, 1:-1]
        + conv_weight[4] * gpad[:, :-2]
    )
    odd = conv_weight[1] * gpad[:, 2:] + conv_weight[3] * gpad[:, 1:-1]
    d_fine = (
        jnp.stack([even, odd], axis=2)
        .reshape(grad.shape[0], 2 * tok_rows, grad.shape[2])
        .astype(jnp.bfloat16)
    )
    partial_grad = jnp.stack([jnp.sum(grad * taps[k], axis=(0, 1)) for k in range(KW)])
    summed = lax.psum(partial_grad, ("dp", "ctx"))
    scale = 1.0 / math.sqrt(lax.axis_size("dp") * tok_rows * ctx_count)
    return (d_fine, summed * scale)


def solution(mesh):
    placed = (
        P("dp", "ctx", None),
        P("dp", "ctx", None),
        P("dp", "ctx", None),
        P("dp", "ctx", None),
        P("dp", "ctx", None),
        P(),
    )
    return jax.shard_map(
        body, mesh=mesh, in_specs=placed, out_specs=(P("dp", "ctx", None), P()), check_vma=False
    )
```

profile of v0, /device:TPU:184, one launch (start us, length us, event | category | flops | bytes accessed | tf_op | source)
XLA Modules:
  0.0 341.5 jit_solution(18383458230890813925)
XLA Ops:
  7.2 0.0 all-gather.3.cloned.1.call-start
  7.2 0.7 all-gather.3.cloned.1.call-update
  7.9 2.2 copy.29
  10.1 0.5 broadcast.15
  10.6 8.8 %reduce.10 = bf16[1536,128]{1,0:T(8,128)(2,1)S(1)} reduce(bf16[1536,1,128]{2,1,0:T(2,128)(2,1)S(1)} %bitcast.34, bf16[]{:T(256)} %broadcast.15), dimensions={1}, to_apply=%bitcast.29.reduce_sub_computation | reduce | bytes 786434
  19.4 0.8 reshape.84
  20.2 0.0 copy-start.1
  20.2 13.8 %all-to-all-start = ((bf16[32,2,3072]{2,1,0:T(2,128)(2,1)}), bf16[32,2,3072]{2,1,0:T(2,128)(2,1)S(1)}, u32[]{:S(2)}, u32[]{:S(2)}) async-start(bf16[32,2,3072]{2,1,0:T(2,128)(2,1)} %reshape.84), calls=%async_computation | async-start | bytes 786432 | tf_op jit(solution)/shard_map/all_to_all | solution.py:53
  34.0 0.0 all-gather.5.cloned.1.call-start
  34.1 0.7 all-gather.5.cloned.1.call-update
  34.8 0.0 copy-start.2
  34.8 12.8 %all-to-all-done = bf16[32,2,3072]{2,1,0:T(2,128)(2,1)S(1)} async-done(((bf16[32,2,3072]{2,1,0:T(2,128)(2,1)}), bf16[32,2,3072]{2,1,0:T(2,128)(2,1)S(1)}, u32[]{:S(2)}, u32[]{:S(2)}) %all-to-all-start) | async-done | bytes 393248 | tf_op jit(solution)/shard_map/all_to_all | solution.py:53
  47.6 0.3 reshape.85
  47.9 0.1 copy.31
  48.0 0.8 rev.6
  48.7 8.5 %all-to-all-start.1 = ((bf16[32,128,48]{1,2,0:T(8,128)(2,1)}), bf16[32,128,48]{1,2,0:T(8,128)(2,1)S(1)}, u32[]{:S(2)}, u32[]{:S(2)}) async-start(bf16[32,128,48]{1,2,0:T(8,128)(2,1)} %rev.6), calls=%async_computation.1 | async-start | bytes 786432 | tf_op jit(solution)/shard_map/all_to_all | solution.py:55
  57.2 0.0 copy-done.1
  57.3 0.3 copy.24
  57.5 5.5 %collective-permute-start = (bf16[1,2,1536]{1,2,0:T(8,128)(2,1)S(1)}, bf16[1,2,1536]{1,2,0:T(8,128)(2,1)}, u32[]{:S(2)}, u32[]{:S(2)}) collective-permute-start(bf16[1,2,1536]{1,2,0:T(8,128)(2,1)S(1)} %copy.24), channel_id=1, source_target_pairs={{0,1},{1,2},{2,3},{3,4},{4,5},{5,6},{6,7},{7,8},{8,9},{9,10},{10,1... | collective-permute-start | bytes 18440 | tf_op jit(solution)/shard_map/ppermute | solution.py:20
  63.0 0.3 copy.25
  63.3 2.1 collective-permute-start.1
  65.4 0.0 copy-done.2
  65.4 0.1 slice_reduce_fusion.4
  65.5 0.3 copy.26
  65.8 1.0 copy.32
  66.8 14.4 %slice.65 = bf16[1,128,1536]{1,2,0:T(8,128)(2,1)S(1)} slice(bf16[1,256,1536]{1,2,0:T(8,128)(2,1)S(1)} %copy.26), slice={[0:1:1], [0:256:2], [0:1536:1]} | slice | bytes 786432 | tf_op jit(solution)/shard_map/slice | solution.py:49
  81.2 0.0 collective-permute-done
  81.2 5.9 %collective-permute-done.1 = bf16[1,2,1536]{1,2,0:T(8,128)(2,1)} collective-permute-done((bf16[1,2,1536]{1,2,0:T(8,128)(2,1)S(1)}, bf16[1,2,1536]{1,2,0:T(8,128)(2,1)}, u32[]{:S(2)}, u32[]{:S(2)}) %collective-permute-start.1) | collective-permute-done | bytes 6176 | tf_op jit(solution)/shard_map/ppermute | solution.py:22
  87.1 1.8 pad_maximum_fusion
  88.9 14.4 %slice.61 = bf16[1,128,1536]{1,2,0:T(8,128)(2,1)S(1)} slice(bf16[1,260,1536]{1,2,0:T(8,128)(2,1)S(1)} %pad_maximum_fusion), slice={[0:1:1], [0:256:2], [0:1536:1]} | slice | bytes 786432 | tf_op jit(solution)/shard_map/slice | solution.py:49
  103.3 14.4 %slice.63 = bf16[1,128,1536]{1,2,0:T(8,128)(2,1)S(1)} slice(bf16[1,260,1536]{1,2,0:T(8,128)(2,1)S(1)} %pad_maximum_fusion), slice={[0:1:1], [1:257:2], [0:1536:1]} | slice | bytes 786432 | tf_op jit(solution)/shard_map/slice | solution.py:49
  117.7 14.7 %slice.67 = bf16[1,128,1536]{1,2,0:T(8,128)(2,1)S(1)} slice(bf16[1,260,1536]{1,2,0:T(8,128)(2,1)S(1)} %pad_maximum_fusion), slice={[0:1:1], [3:259:2], [0:1536:1]} | slice | bytes 786432 | tf_op jit(solution)/shard_map/slice | solution.py:49
  132.4 15.0 %slice.69 = bf16[1,128,1536]{1,2,0:T(8,128)(2,1)} slice(bf16[1,260,1536]{1,2,0:T(8,128)(2,1)S(1)} %pad_maximum_fusion), slice={[0:1:1], [4:260:2], [0:1536:1]} | slice | bytes 786432 | tf_op jit(solution)/shard_map/slice | solution.py:49
  147.4 0.0 all-to-all-done.1
  147.4 1.3 rev.7
  148.7 0.0 all-gather.3.cloned.1.call-done
  148.8 9.3 %multiply_reduce_fusion = (f32[128,8]{0,1:T(8,128)S(1)}, f32[128,8,4096]{2,0,1:T(8,128)}) fusion(bf16[1,4096,128]{2,1,0:T(8,128)(2,1)} %all-gather.3.cloned.1.call-done, bf16[128,8,128]{2,1,0:T(8,128)(2,1)S(1)} %bitcast.36), kind=kOutput, calls=%fused_computation.1 | convolution fusion | flops 1082129408 | bytes 18092032 | tf_op jit(solution)/shard_map/qhd,kd->qhk/dot_general | solution.py:38
  158.0 8.6 %fusion = f32[128,8]{0,1:T(8,128)S(1)} fusion(f32[128,8,4096]{2,0,1:T(8,128)} %get-tuple-element.20, f32[128,8]{0,1:T(8,128)S(1)} %broadcast_maximum_fusion), kind=kLoop, calls=%fused_computation.2 | loop fusion | flops 12581888 | bytes 16785408 | tf_op jit(solution)/shard_map/reduce_sum | solution.py:43
  166.7 0.0 copy-start
  166.7 29.0 %all-gather.5.cloned.1.call-done = bf16[1,4096,192]{1,2,0:T(8,128)(2,1)} async-done(((bf16[1,128,192]{1,2,0:T(8,128)(2,1)}), bf16[1,4096,192]{1,2,0:T(8,128)(2,1)}) %all-gather.5.cloned.1.call-update) | async-done | bytes 1572880 | tf_op jit(solution)/shard_map/all_gather | solution.py:37
  195.6 8.0 %fusion.7 = f32[128,8,192]{0,2,1:T(8,128)S(1)} fusion(bf16[1,4096,192]{1,2,0:T(8,128)(2,1)} %all-gather.5.cloned.1.call-done, f32[128,8,4096]{2,0,1:T(8,128)} %get-tuple-element.20, f32[128,8]{0,1:T(8,128)S(1)} %broadcast_maximum_fusion, f32[128,8]{0,1:T(8,128)S(1)} %fusion), kind=kOutput, calls=%fused_computation.19 | convolution fusion | flops 1623392256 | bytes 19144704 | tf_op jit(solution)/shard_map/qhk,kv->qhv/dot_general | solution.py:44
  203.6 0.0 copy-done
  203.6 2.7 fusion.22
  206.4 0.1 stack.38
  206.5 93.2 %psum.7 = f32[5,1536]{1,0:T(8,128)S(1)} all-reduce(f32[5,1536]{1,0:T(8,128)S(1)} %stack.38), channel_id=1, replica_groups=mesh['dp'=16,'ctx'=32] {'dp','ctx'}, use_global_device_ids=true, to_apply=%region_7.0 | all-reduce | flops 7680 | bytes 61440 | tf_op jit(solution)/shard_map/psum | solution.py:70
  299.7 0.2 fusion.31
  299.9 6.2 %collective-permute-start.2 = (bf16[1,1,1536]{1,2,0:T(8,128)(2,1)S(1)}, bf16[1,1,1536]{1,2,0:T(8,128)(2,1)S(1)}, u32[]{:S(2)}, u32[]{:S(2)}) collective-permute-start(bf16[1,1,1536]{1,2,0:T(8,128)(2,1)S(1)} %get-tuple-element.17), channel_id=1, source_target_pairs={{0,1},{1,2},{2,3},{3,4},{4,5},{5,6},{6,7},{7,8},{8,9},{9,10},{10,1... | collective-permute-start | bytes 9224 | tf_op jit(solution)/shard_map/ppermute | solution.py:20
  306.1 1.9 collective-permute-start.3
  308.0 0.6 broadcast_multiply_fusion
  308.6 11.6 %collective-permute-done.2 = bf16[1,1,1536]{1,2,0:T(8,128)(2,1)S(1)} collective-permute-done((bf16[1,1,1536]{1,2,0:T(8,128)(2,1)S(1)}, bf16[1,1,1536]{1,2,0:T(8,128)(2,1)S(1)}, u32[]{:S(2)}, u32[]{:S(2)}) %collective-permute-start.2) | collective-permute-done | bytes 3104 | tf_op jit(solution)/shard_map/ppermute | solution.py:20
  320.2 10.3 %collective-permute-done.3 = bf16[1,1,1536]{1,2,0:T(8,128)(2,1)S(1)} collective-permute-done((bf16[1,1,1536]{1,2,0:T(8,128)(2,1)S(1)}, bf16[1,1,1536]{1,2,0:T(8,128)(2,1)S(1)}, u32[]{:S(2)}, u32[]{:S(2)}) %collective-permute-start.3) | collective-permute-done | bytes 3104 | tf_op jit(solution)/shard_map/ppermute | solution.py:22
  330.5 0.4 maximum_convert_fusion
  330.9 1.7 fusion.26
  332.6 0.1 pad_maximum_fusion.1
  332.7 0.8 copy.30
  333.5 1.2 convert_element_type.56
  (7 shorter events, 0.0 us)
Async XLA Ops:
  7.2 141.6 %all-gather.3.cloned.1.call-start = ((), (), s32[]{:S(2)}) async-start(), calls=%async_computation.2 | async-start | bytes 1081344 | tf_op jit(solution)/shard_map/all_gather | solution.py:36
  20.2 37.0 %copy-start.1 = (bf16[1,256,1536]{2,1,0:T(8,128)(2,1)S(1)}, bf16[1,256,1536]{2,1,0:T(8,128)(2,1)}, u32[]{:S(2)}) copy-start(bf16[1,256,1536]{2,1,0:T(8,128)(2,1)} %param.9) | copy-start | bytes 2359300
  20.2 27.4 %all-to-all-start = ((bf16[32,2,3072]{2,1,0:T(2,128)(2,1)}), bf16[32,2,3072]{2,1,0:T(2,128)(2,1)S(1)}, u32[]{:S(2)}, u32[]{:S(2)}) async-start(bf16[32,2,3072]{2,1,0:T(2,128)(2,1)} %reshape.84), calls=%async_computation | async-start | bytes 786432 | tf_op jit(solution)/shard_map/all_to_all | solution.py:53
  34.0 161.6 %all-gather.5.cloned.1.call-start = ((), (), s32[]{:S(2)}) async-start(), calls=%async_computation.3 | async-start | bytes 1622016 | tf_op jit(solution)/shard_map/all_gather | solution.py:37
  34.8 30.6 %copy-start.2 = (f32[5,1536]{1,0:T(8,128)S(1)}, f32[5,1536]{1,0:T(8,128)}, u32[]{:S(2)}) copy-start(f32[5,1536]{1,0:T(8,128)} %param.11) | copy-start | bytes 92164
  48.7 98.6 %all-to-all-start.1 = ((bf16[32,128,48]{1,2,0:T(8,128)(2,1)}), bf16[32,128,48]{1,2,0:T(8,128)(2,1)S(1)}, u32[]{:S(2)}, u32[]{:S(2)}) async-start(bf16[32,128,48]{1,2,0:T(8,128)(2,1)} %rev.6), calls=%async_computation.1 | async-start | bytes 786432 | tf_op jit(solution)/shard_map/all_to_all | solution.py:55
  57.5 23.6 %collective-permute-start = (bf16[1,2,1536]{1,2,0:T(8,128)(2,1)S(1)}, bf16[1,2,1536]{1,2,0:T(8,128)(2,1)}, u32[]{:S(2)}, u32[]{:S(2)}) collective-permute-start(bf16[1,2,1536]{1,2,0:T(8,128)(2,1)S(1)} %copy.24), channel_id=1, source_target_pairs={{0,1},{1,2},{2,3},{3,4},{4,5},{5,6},{6,7},{7,8},{8,9},{9,10},{10,1... | collective-permute-start | bytes 18440 | tf_op jit(solution)/shard_map/ppermute | solution.py:20
  63.3 23.8 %collective-permute-start.1 = (bf16[1,2,1536]{1,2,0:T(8,128)(2,1)S(1)}, bf16[1,2,1536]{1,2,0:T(8,128)(2,1)}, u32[]{:S(2)}, u32[]{:S(2)}) collective-permute-start(bf16[1,2,1536]{1,2,0:T(8,128)(2,1)S(1)} %copy.25), channel_id=1, source_target_pairs={{1,0},{2,1},{3,2},{4,3},{5,4},{6,5},{7,6},{8,7},{9,8},{10,9},{11,1... | collective-permute-start | bytes 18440 | tf_op jit(solution)/shard_map/ppermute | solution.py:22
  166.7 36.9 %copy-start = (bf16[1,128,1536]{1,2,0:T(8,128)(2,1)S(1)}, bf16[1,128,1536]{1,2,0:T(8,128)(2,1)}, u32[]{:S(2)}) copy-start(bf16[1,128,1536]{1,2,0:T(8,128)(2,1)} %slice.69) | copy-start | bytes 1179652
  299.9 20.3 %collective-permute-start.2 = (bf16[1,1,1536]{1,2,0:T(8,128)(2,1)S(1)}, bf16[1,1,1536]{1,2,0:T(8,128)(2,1)S(1)}, u32[]{:S(2)}, u32[]{:S(2)}) collective-permute-start(bf16[1,1,1536]{1,2,0:T(8,128)(2,1)S(1)} %get-tuple-element.17), channel_id=1, source_target_pairs={{0,1},{1,2},{2,3},{3,4},{4,5},{5,6},{6,7},{7,8},{8,9},{9,10},{10,1... | collective-permute-start | bytes 9224 | tf_op jit(solution)/shard_map/ppermute | solution.py:20
  306.1 24.4 %collective-permute-start.3 = (bf16[1,1,1536]{1,2,0:T(8,128)(2,1)S(1)}, bf16[1,1,1536]{1,2,0:T(8,128)(2,1)S(1)}, u32[]{:S(2)}, u32[]{:S(2)}) collective-permute-start(bf16[1,1,1536]{1,2,0:T(8,128)(2,1)S(1)} %get-tuple-element.18), channel_id=1, source_target_pairs={{1,0},{2,1},{3,2},{4,3},{5,4},{6,5},{7,6},{8,7},{9,8},{10,9},{11,1... | collective-permute-start | bytes 9224 | tf_op jit(solution)/shard_map/ppermute | solution.py:22
Sparse Core Ops, SparseCore 0:
  11.2 102.2 all-gather.2
  116.5 79.0 all-gather.4
where the time goes:
time: 342 us; the launch traced here: 341 us
  blocking collectives  93.2 us (27%)
  local copies, waits for them, and re-layouts  82.9 us (24%)
  waiting for transfers between devices  70.9 us (21%)
  starting transfers between devices  38.1 us (11%)
  other arithmetic  24.9 us (7%)
  matrix products  17.2 us (5%)
  between operations  14.3 us (4%)
    psum x1, blocking collectives, body(): summed = lax.psum(partial_grad, ('dp', 'ctx'))  93.2 us
    slice x5, local copies, waits for them, and re-layouts, body(): padded[:, k:k + 2 * tok_rows:2, :].astype(jnp.float32)  72.8 us
    all_gather x1, waiting for transfers between devices, body(): value_piece = lax.all_gather(values, 'ctx', axis=1, tiled=True)  29 us
    ppermute x2, waiting for transfers between devices, padded_2(): lax.ppermute(head, axis, [((i + 1) % count, i) for i in range(ends)])  16.2 us
    all_to_all x1, starting transfers between devices, body(): lax.all_to_all(rc_state, 'ctx', split_axis=2, concat_axis=0, tiled=True)  13.8 us
    all_to_all x1, waiting for transfers between devices, body(): lax.all_to_all(rc_state, 'ctx', split_axis=2, concat_axis=0, tiled=True)  12.8 us
    ppermute x2, starting transfers between devices, padded_2(): lax.ppermute(tail, axis, [(i, (i + 1) % count) for i in range(ends)])  11.7 us
    ppermute x2, waiting for transfers between devices, padded_2(): lax.ppermute(tail, axis, [(i, (i + 1) % count) for i in range(ends)])  11.6 us
  transfers between devices with their start and end apart: 8, of which 5 were waited for; matrix products, arithmetic and copies ran while one was open for 32% of the time, Pallas kernels for 0%

commit v1 on v0

v1 whole, which is shorter than its diff:
```python
import functools
import heapq
import math

import jax
import jax.numpy as jnp
from jax import lax
from jax.experimental import pallas as pl
from jax.experimental.pallas import tpu as pltpu
from jax.sharding import PartitionSpec as P

HEADS = 8
DK = 128
DV = 192
VROWS = DV
ROWS = 128
D = HEADS * DV
KW = 5
NA, NY = 4, 8
MESH = pl.DeviceIdType.MESH
F32 = jnp.float32
BF16 = jnp.bfloat16


def block_sends():
    sends = {}
    for da in range(NA):
        cw = 4 - da % 2
        for dy in range(NY):
            behind = (NY - dy) % NY
            v, k = [], []
            if dy == 0:
                if da == 0:
                    v += [("a+", ("V", 3, 0)), ("a-", ("V", 1, 0)), ("a2", ("V", 2, 0))]
                v += [("y+", ("V", da, 7)), ("y-", ("V", da, 1))]
            elif behind <= cw:
                if behind < cw:
                    v.append(("y+", ("V", da, dy - 1)))
            elif dy < 7 - cw:
                v.append(("y-", ("V", da, dy + 1)))
            sends[("V", da, dy)] = v
            if da == 0:
                if dy == 0:
                    k += [("y+", ("K", 0, 7)), ("y-", ("K", 0, 1))]
                elif behind < 4:
                    k.append(("y+", ("K", 0, dy - 1)))
                elif dy < 3:
                    k.append(("y-", ("K", 0, dy + 1)))
                k += [("a+", ("K", 3, dy)), ("a-", ("K", 1, dy))]
            elif da == 3 and dy % 2 == 0:
                k.append(("a+", ("K", 2, dy)))
            elif da == 1 and dy % 2 == 1:
                k.append(("a-", ("K", 2, dy)))
            sends[("K", da, dy)] = k
    return sends


def arrival_order(sends):
    free = {"y+": 0.0, "y-": 0.0, "a+": 0.0, "a-": 0.0}
    cost = {"V": 1.06, "K": 0.71}
    queue = [(0.0, 0, ("K", 0, 0)), (0.0, 1, ("V", 0, 0))]
    order, n = [], 2
    while queue:
        now, _, key = heapq.heappop(queue)
        order.append(key)
        for link, child in sends[key]:
            if link == "a2":
                end = max(now, free["a+"], free["a-"]) + 2 * cost[key[0]]
                free["a+"] = free["a-"] = end
                late = 3.6
            else:
                along_y = link[0] == "y"
                end = max(now, free[link]) + cost[key[0]] * (1 if along_y else 2)
                free[link] = end
                late = 1.8 if along_y else 2.4
            heapq.heappush(queue, (end + late, n, child))
            n += 1
    return order


def kernel(
    q_ref, k_ref, v_ref, ff_ref, rc_ref, w_ref, df_ref, dw_ref,
    kbuf, vbuf, rcin, qs, vx, top, acc, wide, base, ev, od, grd, halo_out, halo_in, edge_out, edge_in,
    send_sem, k_sem, v_sem, m_send, m_recv, h_send, h_recv, e_send, e_recv,
):
    dp, ctx = lax.axis_index("dp"), lax.axis_index("ctx")
    a, y = ctx // NY, lax.rem(ctx, NY)
    count = NA * NY

    def at(a_new, y_new):
        return (dp, lax.rem(a_new, NA) * NY + lax.rem(y_new, NY))

    right, left = (dp, lax.rem(ctx + 1, count)), (dp, lax.rem(ctx + count - 1, count))
    mirror = (dp, count - 1 - ctx)
    peers = {
        "y+": at(a, y + 1), "y-": at(a, y + NY - 1), "a+": at(a + 1, y), "a-": at(a + NA - 1, y), "a2": at(a + 2, y),
    }
    barrier = pltpu.get_barrier_semaphore()
    greeted = list(peers.values()) + [right, left, mirror]
    for peer in greeted:
        pl.semaphore_signal(barrier, inc=1, device_id=peer, device_id_type=MESH)

    kbuf[y, a] = k_ref[...]
    v_own = v_ref[...]
    tail = v_own[:, 128:]
    vbuf[y, a, 0:ROWS, :] = v_own[:, :128]
    vbuf[y, a, ROWS:VROWS, :] = jnp.concatenate([tail[:64], tail[64:]], axis=1)

    def widen(i, _):
        cols = pl.ds(pl.multiple_of(i * 128, 128), 128)
        wide[i] = ff_ref[:, cols].astype(F32)
        return 0

    lax.fori_loop(0, D // 128, widen, 0)
    halo_out[0] = ff_ref[2 * ROWS - 16 : 2 * ROWS, :].astype(F32)[14:16]
    halo_out[1] = ff_ref[0:16, :].astype(F32)[0:2]
    pl.semaphore_wait(barrier, len(greeted))

    halo = [
        pltpu.make_async_remote_copy(
            halo_out.at[i], halo_in.at[i], h_send.at[i], h_recv.at[i], device_id=peer, device_id_type=MESH
        )
        for i, peer in enumerate((right, left))
    ]
    mirrored = pltpu.make_async_remote_copy(rc_ref, rcin, m_send, m_recv, device_id=mirror, device_id_type=MESH)

    sends = block_sends()
    order = arrival_order(sends)
    started = []

    def block(key):
        o_a, o_y = lax.rem(a + key[1], NA), lax.rem(y + key[2], NY)
        buf, sem = (kbuf, k_sem) if key[0] == "K" else (vbuf, v_sem)
        return buf.at[o_y, o_a], sem.at[o_y, o_a]

    def event(key):
        ref, sem = block(key)
        if key[1:] != (0, 0):
            pltpu.make_async_remote_copy(
                ref, ref, sem, sem, device_id=peers["y+"], device_id_type=MESH
            ).wait_recv()
        for link, _ in sends[key]:
            copy = pltpu.make_async_remote_copy(
                ref, ref, send_sem.at[len(started)], sem, device_id=peers[link], device_id_type=MESH
            )
            copy.start()
            started.append(copy)

    def prepare():
        def heads(h, _):
            qs[h] = q_ref[:, pl.ds(pl.multiple_of(h * DK, DK), DK)]
            top[h] = jnp.full((ROWS, 128), -1e30, F32)
            acc[h] = jnp.zeros((ROWS, 256), F32)
            return 0

        lax.fori_loop(0, HEADS, heads, 0)
        lane = lax.broadcasted_iota(jnp.int32, (NA * ROWS, 128), 1)
        vx[:, 128:256] = jnp.where(lane < 64, 0.0, 1.0).astype(BF16)

    def gather_values(dy):
        o_y = lax.rem(y + dy, NY)
        for i in range(NA):
            vx[i * ROWS : (i + 1) * ROWS, 0:128] = vbuf[o_y, i, 0:ROWS, :]
            packed = vbuf[o_y, i, ROWS:VROWS, :]
            vx[i * ROWS : i * ROWS + 64, 128:192] = packed[:, :64]
            vx[i * ROWS + 64 : (i + 1) * ROWS, 128:192] = packed[:, 64:]

    factor = DK ** (-0.5) * math.log2(math.e)

    def attend(dy, low, high):
        o_y = lax.rem(y + dy, NY)

        def head(h, _):
            keys = kbuf[o_y].reshape(NA * ROWS, DK)
            s = lax.dot_general(qs[h], keys, (((1,), (1,)), ((), ())), preferred_element_type=F32)
            old = top[h]
            new = jnp.maximum(old, jnp.max(s, axis=1, keepdims=True))
            p = jnp.exp2((s - new[:, :1]) * factor).astype(BF16)
            fade = jnp.exp2((old - new) * factor)
            fade = jnp.concatenate([fade, fade], axis=1)
            acc[h] = acc[h] * fade + jnp.dot(p, vx[...], preferred_element_type=F32)
            top[h] = new
            return 0

        lax.fori_loop(low, high, head, 0)

    def convolve():
        for copy in halo:
            copy.wait_recv()
        inner_left = jnp.where(ctx > 0, 1.0, 0.0)
        inner_right = jnp.where(ctx < count - 1, 1.0, 0.0)
        ev[7:8, :] = halo_in[0, 0:1, :] * inner_left
        od[7:8, :] = halo_in[0, 1:2, :] * inner_left
        ev[136:137, :] = halo_in[1, 0:1, :] * inner_right

        def chunk(i, _):
            cols = pl.ds(pl.multiple_of(i * 128, 128), 128)
            ev[8:136, cols] = wide[i, pl.ds(0, ROWS, stride=2), :]
            od[8:136, cols] = wide[i, pl.ds(1, ROWS, stride=2), :]
            w = w_ref[:, cols]
            base[:, cols] = (
                w[0:1] * ev[7:135, cols]
                + w[1:2] * od[7:135, cols]
                + w[2:3] * ev[8:136, cols]
                + w[3:4] * od[8:136, cols]
                + w[4:5] * ev[9:137, cols]
            )
            return 0

        lax.fori_loop(0, D // 128, chunk, 0)

    ready, done = [], {}
    for n, key in enumerate(order):
        event(key)
        if n == 1:
            for copy in halo:
                copy.start()
            mirrored.start()
            prepare()
        if n == 9:
            convolve()
        done[key[2]] = done.get(key[2], 0) + 1
        if done[key[2]] == 2 * NA:
            ready += [(key[2], h) for h in range(0, HEADS, 2)]
        if n < len(order) - 1 and ready:
            dy, h = ready.pop(0)
            if h == 0:
                gather_values(dy)
            attend(dy, h, h + 2)
    while ready:
        dy, h = ready[0]
        if h == 0:
            gather_values(dy)
        attend(dy, h, HEADS)
        ready = [r for r in ready if r[0] != dy]

    mirrored.wait_recv()
    row = lax.broadcasted_iota(jnp.int32, (ROWS, ROWS), 0)
    col = lax.broadcasted_iota(jnp.int32, (ROWS, ROWS), 1)
    turn = jnp.where(row + col == ROWS - 1, 1.0, 0.0).astype(BF16)

    def finish(j, _):
        cols = pl.ds(pl.multiple_of(j * 2 * DV, 128), 2 * DV)
        one, two = acc[2 * j], acc[2 * j + 1]
        attended = jnp.concatenate(
            [one[:, :DV] / one[:, DV : DV + 1], two[:, :DV] / two[:, DV : DV + 1]], axis=1
        )
        grd[8:136, cols] = base[:, cols] + attended - jnp.dot(turn, rcin[:, cols], preferred_element_type=F32)
        return 0

    lax.fori_loop(0, HEADS // 2, finish, 0)
    edge_out[0] = grd[135:136, :]
    edge_out[1] = grd[8:9, :]
    edges = [
        pltpu.make_async_remote_copy(
            edge_out.at[i], edge_in.at[i], e_send.at[i], e_recv.at[i], device_id=peer, device_id_type=MESH
        )
        for i, peer in enumerate((right, left))
    ]
    for copy in edges:
        copy.start()

    def weigh(i, _):
        cols = pl.ds(pl.multiple_of(i * 128, 128), 128)
        g = grd[8:136, cols]
        taps = (ev[7:135, cols], od[7:135, cols], ev[8:136, cols], od[8:136, cols], ev[9:137, cols])
        dw_ref[:, cols] = jnp.concatenate([jnp.sum(g * tap, axis=0, keepdims=True) for tap in taps], axis=0)
        return 0

    lax.fori_loop(0, D // 128, weigh, 0)
    for copy in edges:
        copy.wait_recv()
    grd[7:8, :] = edge_in[0] * jnp.where(ctx > 0, 1.0, 0.0)
    grd[136:137, :] = edge_in[1] * jnp.where(ctx < count - 1, 1.0, 0.0)

    def spread(i, _):
        cols = pl.ds(pl.multiple_of(i * 128, 128), 128)
        w = w_ref[:, cols]
        before, here, after = grd[7:135, cols], grd[8:136, cols], grd[9:137, cols]
        wide[i, pl.ds(0, ROWS, stride=2), :] = w[0:1] * after + w[2:3] * here + w[4:5] * before
        wide[i, pl.ds(1, ROWS, stride=2), :] = w[1:2] * after + w[3:4] * here
        df_ref[:, cols] = wide[i].astype(BF16)
        return 0

    lax.fori_loop(0, D // 128, spread, 0)
    for copy in started + halo + edges + [mirrored]:
        copy.wait_send()


def run(queries, keys, values, features_fine, rc_state, conv_weight):
    vmem = pl.BlockSpec(memory_space=pltpu.VMEM)
    dma = pltpu.SemaphoreType.DMA
    n_sends = sum(len(s) for s in block_sends().values())
    return pl.pallas_call(
        kernel,
        name="attend_and_convolve",
        out_shape=(jax.ShapeDtypeStruct((2 * ROWS, D), BF16), jax.ShapeDtypeStruct((KW, D), F32)),
        in_specs=[vmem] * 6,
        out_specs=(vmem, vmem),
        scratch_shapes=[
            pltpu.VMEM((NY, NA, ROWS, DK), BF16),
            pltpu.VMEM((NY, NA, VROWS, 128), BF16),
            pltpu.VMEM((ROWS, D), BF16),
            pltpu.VMEM((HEADS, ROWS, DK), BF16),
            pltpu.VMEM((NA * ROWS, 256), BF16),
            pltpu.VMEM((HEADS, ROWS, 128), F32),
            pltpu.VMEM((HEADS, ROWS, 256), F32),
            pltpu.VMEM((D // 128, 2 * ROWS, 128), F32),
            pltpu.VMEM((ROWS, D), F32),
            pltpu.VMEM((ROWS + 16, D), F32),
            pltpu.VMEM((ROWS + 16, D), F32),
            pltpu.VMEM((ROWS + 16, D), F32),
            pltpu.VMEM((2, 2, D), F32),
            pltpu.VMEM((2, 2, D), F32),
            pltpu.VMEM((2, 1, D), F32),
            pltpu.VMEM((2, 1, D), F32),
            dma((n_sends,)),
            dma((NY, NA)),
            dma((NY, NA)),
            dma,
            dma,
            dma((2,)),
            dma((2,)),
            dma((2,)),
            dma((2,)),
        ],
        compiler_params=pltpu.CompilerParams(
            collective_id=0, has_side_effects=True, vmem_limit_bytes=40 * 2**20
        ),
        cost_estimate=pl.CostEstimate(flops=2_700_000_000, bytes_accessed=4_000_000, transcendentals=4_200_000),
    )(queries, keys, values, features_fine, rc_state, conv_weight)


def body(queries, keys, values, features_fine, rc_state, conv_weight):
    d_fine, partial = run(queries[0], keys[0], values[0], features_fine[0], rc_state[0], conv_weight)
    summed = lax.psum(partial, ("dp", "ctx"))
    scale = 1.0 / math.sqrt(lax.axis_size("dp") * lax.axis_size("ctx") * ROWS)
    return d_fine[None], summed * scale


def solution(mesh):
    split = P("dp", "ctx", None)
    return jax.shard_map(
        body, mesh=mesh, in_specs=(split,) * 5 + (P(),), out_specs=(split, P()), check_vma=False
    )
```

time: 342 us -> 198 us (0.58)
  the two profiles are of different devices: /device:TPU:184 before, /device:TPU:1 now
where the time goes in v1:
time: 198 us
  blocking collectives  105 us (53%)
  Pallas kernels  86.3 us (44%)
  local copies, waits for them, and re-layouts  4.88 us (2%)
    psum x1, blocking collectives, body(): summed = lax.psum(partial, ('dp', 'ctx'))  105 us
    pallas_call x1, Pallas kernels, run(): pl.pallas_call(kernel, name='attend_and_convolve', out_shape=(jax.ShapeDt...  86.3 us
    unnamed x12, local copies, waits for them, and re-layouts  4.88 us

profile of v1, /device:TPU:1, one launch (start us, length us, event | category | flops | bytes accessed | tf_op | source)
XLA Modules:
  0.0 197.8 jit_solution(10096227748956635248)
XLA Ops:
  0.6 0.0 copy-start.3
  0.6 0.0 copy-start.4
  0.7 0.9 copy.8
  1.6 0.0 copy-done.3
  1.6 0.0 copy-done.4
  1.6 0.0 copy-start
  1.6 1.1 copy-done
  2.7 0.0 copy-start.1
  2.7 1.0 copy-done.1
  3.7 0.0 copy-start.2
  3.7 0.9 copy-done.2
  4.7 86.3 %attend_and_convolve.1 = (bf16[256,1536]{1,0:T(8,128)(2,1)S(1)}, f32[5,1536]{1,0:T(8,128)S(1)}) custom-call(bf16[128,1024]{1,0:T(8,128)(2,1)S(1)} %bitcast.10, bf16[128,128]{1,0:T(8,128)(2,1)S(1)} %bitcast.11, bf16[128,192]{1,0:T(8,128)(2,1)S(1)} %bitcast.7, bf16[256,1536]{1,0:T(8,128)(2,1)S(1)} %bitcast.8, bf16[128,1536]{1,0:T(8,128)(2,1)S(1)} %bitcast.9, ...), custom_call_target="tpu_custom_call" | custom-call | flops 2700000000 | bytes 4000000 | tf_op jit(solution)/shard_map/attend_and_convolve/pallas_call | solution.py:294
  91.0 105.3 %psum.7 = f32[5,1536]{1,0:T(8,128)S(1)} all-reduce(f32[5,1536]{1,0:T(8,128)S(1)} %get-tuple-element.5), channel_id=1, replica_groups=mesh['dp'=16,'ctx'=32] {'dp','ctx'}, use_global_device_ids=true, to_apply=%region_0.0 | all-reduce | flops 7680 | bytes 61440 | tf_op jit(solution)/shard_map/psum | solution.py:336
  196.3 0.6 broadcast_multiply_fusion
  196.9 0.9 copy.10
Async XLA Ops:
  0.6 0.9 copy-start.3
  0.6 0.9 copy-start.4
  1.6 1.1 copy-start
  2.7 1.0 copy-start.1
  3.7 0.9 copy-start.2

commit v2 on v1

v2 whole, which is shorter than its diff:
```python
import heapq
import math

import jax
import jax.numpy as jnp
from jax import lax
from jax.experimental import pallas as pl
from jax.experimental.pallas import tpu as pltpu
from jax.sharding import PartitionSpec as P

HEADS = 8
DK = 128
DV = 192
ROWS = 128
D = HEADS * DV
KW = 5
NA, NY = 4, 8
NX, NZ = 4, 8
MESH = pl.DeviceIdType.MESH
F32 = jnp.float32
BF16 = jnp.bfloat16


def block_sends():
    sends = {}
    for da in range(NA):
        cw = 4 - da % 2
        for dy in range(NY):
            behind = (NY - dy) % NY
            v, k = [], []
            if dy == 0:
                if da == 0:
                    v += [("a+", ("V", 3, 0)), ("a-", ("V", 1, 0)), ("a2", ("V", 2, 0))]
                v += [("y+", ("V", da, 7)), ("y-", ("V", da, 1))]
            elif behind <= cw:
                if behind < cw:
                    v.append(("y+", ("V", da, dy - 1)))
            elif dy < 7 - cw:
                v.append(("y-", ("V", da, dy + 1)))
            sends[("V", da, dy)] = v
            if da == 0:
                if dy == 0:
                    k += [("y+", ("K", 0, 7)), ("y-", ("K", 0, 1))]
                elif behind < 4:
                    k.append(("y+", ("K", 0, dy - 1)))
                elif dy < 3:
                    k.append(("y-", ("K", 0, dy + 1)))
                k += [("a+", ("K", 3, dy)), ("a-", ("K", 1, dy))]
            elif da == 3 and dy % 2 == 0:
                k.append(("a+", ("K", 2, dy)))
            elif da == 1 and dy % 2 == 1:
                k.append(("a-", ("K", 2, dy)))
            sends[("K", da, dy)] = k
    return sends


def arrival_order(sends):
    free = {"y+": 0.0, "y-": 0.0, "a+": 0.0, "a-": 0.0}
    cost = {"V": 1.06, "K": 0.71}
    queue = [(0.0, 0, ("K", 0, 0)), (0.0, 1, ("V", 0, 0))]
    order, n = [], 2
    while queue:
        now, _, key = heapq.heappop(queue)
        order.append(key)
        for link, child in sends[key]:
            if link == "a2":
                end = max(now, free["a+"], free["a-"]) + 2 * cost[key[0]]
                free["a+"] = free["a-"] = end
                late = 3.6
            else:
                along_y = link[0] == "y"
                end = max(now, free[link]) + cost[key[0]] * (1 if along_y else 2)
                free[link] = end
                late = 1.8 if along_y else 2.4
            heapq.heappush(queue, (end + late, n, child))
            n += 1
    return order


def kernel(
    q_ref, k_ref, v_ref, ff_ref, rc_ref, w_ref, df_ref, dw_ref,
    kbuf, vbuf, rcin, qs, kx, vx, top, acc, fine, wide, base, ev, od, grd, halo_out, halo_in, edge_out, edge_in,
    part, core_in, x_in, z_in, y_in, final,
    local, send_sem, k_sem, v_sem, m_recv, h_recv, e_recv, c_recv, x_recv, z_recv, y_recv,
):
    dp, ctx = lax.axis_index("dp"), lax.axis_index("ctx")
    a, y = ctx // NY, lax.rem(ctx, NY)
    core, zlo, x = lax.rem(dp, 2), lax.rem(dp // 2, 2), dp // 4
    z = a * 2 + zlo
    count = NA * NY

    def at(a_new, y_new):
        return (dp, lax.rem(a_new, NA) * NY + lax.rem(y_new, NY))

    right, left = (dp, lax.rem(ctx + 1, count)), (dp, lax.rem(ctx + count - 1, count))
    mirror = (dp, count - 1 - ctx)
    peers = {
        "y+": at(a, y + 1), "y-": at(a, y + NY - 1), "a+": at(a + 1, y), "a-": at(a + NA - 1, y), "a2": at(a + 2, y),
    }
    other_core = (dp + 1 - 2 * core, ctx)
    x_peers = [(lax.rem(x + i, NX) * 4 + zlo * 2 + core, ctx) for i in range(1, NX)]
    z_peers = []
    for i in range(1, NZ):
        z_new = lax.rem(z + i, NZ)
        z_peers.append((x * 4 + lax.rem(z_new, 2) * 2 + core, z_new // 2 * NY + y))
    y_peers = [at(a, y + i) for i in range(1, NY)]
    barrier = pltpu.get_barrier_semaphore()
    greeted = [right, left, mirror, other_core] + x_peers + z_peers + y_peers
    for peer in greeted:
        pl.semaphore_signal(barrier, inc=1, device_id=peer, device_id_type=MESH)

    own_k = pltpu.make_async_copy(k_ref, kbuf.at[y, a], local.at[0])
    own_v = pltpu.make_async_copy(v_ref, vbuf.at[y, a, pl.ds(0, DV)], local.at[1])
    own_f = pltpu.make_async_copy(ff_ref, fine, local.at[2])
    own_q = [
        pltpu.make_async_copy(q_ref.at[:, pl.ds(h * DK, DK)], qs.at[h], local.at[3 + h]) for h in range(HEADS)
    ]
    for copy in [own_f, own_k, own_v] + own_q:
        copy.start()

    started = []

    def push(src, dst, recv_sem, peer):
        copy = pltpu.make_async_remote_copy(
            src, dst, send_sem.at[len(started)], recv_sem, device_id=peer, device_id_type=MESH
        )
        copy.start()
        started.append(copy)

    def landed(ref, sem):
        pltpu.make_async_remote_copy(ref, ref, sem, sem, device_id=other_core, device_id_type=MESH).wait_recv()

    sends = block_sends()
    order = arrival_order(sends)

    def event(key):
        o_a, o_y = lax.rem(a + key[1], NA), lax.rem(y + key[2], NY)
        if key[0] == "K":
            ref, sem = kbuf.at[o_y, o_a], k_sem.at[o_y, o_a]
        else:
            ref, sem = vbuf.at[o_y, o_a, pl.ds(0, DV)], v_sem.at[o_y, o_a]
        if key[1:] != (0, 0):
            landed(ref, sem)
        for link, _ in sends[key]:
            push(ref, ref, sem, peers[link])

    def prepare():
        def heads(h, _):
            top[h] = jnp.full((ROWS, 128), -1e30, F32)
            acc[h] = jnp.zeros((ROWS, 256), F32)
            return 0

        lax.fori_loop(0, HEADS, heads, 0)
        vx[:, DV:256] = jnp.ones((NA * ROWS, 64), BF16)

    def gather_keys(dy):
        o_y = lax.rem(y + dy, NY)
        for i in range(NA):
            rows = slice(i * ROWS, (i + 1) * ROWS)
            kx[:, rows] = kbuf[o_y, i].T
            vx[rows, 0:128] = vbuf[o_y, i, 0:128, :].T
            vx[rows, 128:192] = vbuf[o_y, i, 128:192, :].T

    factor = DK ** (-0.5) * math.log2(math.e)

    def attend(low, high):
        def head(h, _):
            s = jnp.dot(qs[h], kx[...], preferred_element_type=F32)
            old = top[h]
            new = jnp.maximum(old, jnp.max(s, axis=1, keepdims=True))
            p = jnp.exp2((s - new[:, :1]) * factor).astype(BF16)
            fade = jnp.exp2((old - new) * factor)
            fade = jnp.concatenate([fade, fade], axis=1)
            acc[h] = acc[h] * fade + jnp.dot(p, vx[...], preferred_element_type=F32)
            top[h] = new
            return 0

        lax.fori_loop(low, high, head, 0)

    def convolve():
        landed(halo_in.at[0], h_recv.at[0])
        landed(halo_in.at[1], h_recv.at[1])
        inner_left = jnp.where(ctx > 0, 1.0, 0.0)
        inner_right = jnp.where(ctx < count - 1, 1.0, 0.0)
        ev[7:8, :] = halo_in[0, 0:1, :] * inner_left
        od[7:8, :] = halo_in[0, 1:2, :] * inner_left
        ev[136:137, :] = halo_in[1, 0:1, :] * inner_right

        def chunk(i, _):
            cols = pl.ds(pl.multiple_of(i * 128, 128), 128)
            wide[i] = fine[:, cols].astype(F32)
            ev[8:136, cols] = wide[i, pl.ds(0, ROWS, stride=2), :]
            od[8:136, cols] = wide[i, pl.ds(1, ROWS, stride=2), :]
            w = w_ref[:, cols]
            base[:, cols] = (
                w[0:1] * ev[7:135, cols]
                + w[1:2] * od[7:135, cols]
                + w[2:3] * ev[8:136, cols]
                + w[3:4] * od[8:136, cols]
                + w[4:5] * ev[9:137, cols]
            )
            return 0

        lax.fori_loop(0, D // 128, chunk, 0)

    own_f.wait()
    halo_out[0] = fine[2 * ROWS - 16 : 2 * ROWS, :].astype(F32)[14:16]
    halo_out[1] = fine[0:16, :].astype(F32)[0:2]
    own_k.wait()
    own_v.wait()
    pl.semaphore_wait(barrier, len(greeted))

    ready, done = [], {}
    for n, key in enumerate(order):
        event(key)
        if n == 1:
            push(halo_out.at[0], halo_in.at[0], h_recv.at[0], right)
            push(halo_out.at[1], halo_in.at[1], h_recv.at[1], left)
            push(rc_ref, rcin, m_recv, mirror)
            for copy in own_q:
                copy.wait()
            prepare()
        if n == 9:
            convolve()
        done[key[2]] = done.get(key[2], 0) + 1
        if done[key[2]] == 2 * NA:
            ready += [(key[2], h) for h in range(0, HEADS, 2)]
        if n < len(order) - 1 and ready:
            dy, h = ready.pop(0)
            if h == 0:
                gather_keys(dy)
            attend(h, h + 2)
    while ready:
        dy, h = ready[0]
        if h == 0:
            gather_keys(dy)
        attend(h, HEADS)
        ready = [r for r in ready if r[0] != dy]

    landed(rcin, m_recv)
    row = lax.broadcasted_iota(jnp.int32, (ROWS, ROWS), 0)
    col = lax.broadcasted_iota(jnp.int32, (ROWS, ROWS), 1)
    turn = jnp.where(row + col == ROWS - 1, 1.0, 0.0).astype(BF16)

    def finish(j, _):
        cols = pl.ds(pl.multiple_of(j * 2 * DV, 128), 2 * DV)
        one, two = acc[2 * j], acc[2 * j + 1]
        attended = jnp.concatenate(
            [one[:, :DV] / one[:, DV : DV + 1], two[:, :DV] / two[:, DV : DV + 1]], axis=1
        )
        grd[8:136, cols] = base[:, cols] + attended - jnp.dot(turn, rcin[:, cols], preferred_element_type=F32)
        return 0

    lax.fori_loop(0, HEADS // 2, finish, 0)
    edge_out[0] = grd[135:136, :]
    edge_out[1] = grd[8:9, :]
    push(edge_out.at[0], edge_in.at[0], e_recv.at[0], right)
    push(edge_out.at[1], edge_in.at[1], e_recv.at[1], left)

    part[:, 30:32, :] = jnp.zeros((2, 2, 128), F32)
    for half in range(2):
        for j in range(6):
            cols = slice((half * 6 + j) * 128, (half * 6 + j + 1) * 128)
            g = grd[8:136, cols]
            taps = (ev[7:135, cols], od[7:135, cols], ev[8:136, cols], od[8:136, cols], ev[9:137, cols])
            part[half, j * KW : (j + 1) * KW, :] = jnp.concatenate(
                [jnp.sum(g * tap, axis=0, keepdims=True) for tap in taps], axis=0
            )
    push(part.at[1 - core], core_in, c_recv.at[0], other_core)

    def spread(low, high):
        def chunk(i, _):
            cols = pl.ds(pl.multiple_of(i * 128, 128), 128)
            w = w_ref[:, cols]
            before, here, after = grd[7:135, cols], grd[8:136, cols], grd[9:137, cols]
            wide[i, pl.ds(0, ROWS, stride=2), :] = w[0:1] * after + w[2:3] * here + w[4:5] * before
            wide[i, pl.ds(1, ROWS, stride=2), :] = w[1:2] * after + w[3:4] * here
            df_ref[:, cols] = wide[i].astype(BF16)
            return 0

        lax.fori_loop(low, high, chunk, 0)

    landed(core_in, c_recv.at[0])
    x_in[x] = part[core] + core_in[...]
    for i, peer in enumerate(x_peers):
        push(x_in.at[x], x_in.at[x], x_recv.at[x], peer)
    landed(edge_in.at[0], e_recv.at[0])
    landed(edge_in.at[1], e_recv.at[1])
    grd[7:8, :] = edge_in[0] * jnp.where(ctx > 0, 1.0, 0.0)
    grd[136:137, :] = edge_in[1] * jnp.where(ctx < count - 1, 1.0, 0.0)
    spread(0, 3)
    for i in range(1, NX):
        slot = lax.rem(x + i, NX)
        landed(x_in.at[slot], x_recv.at[slot])
    z_in[z] = jnp.sum(x_in[...], axis=0)
    for peer in z_peers:
        push(z_in.at[z], z_in.at[z], z_recv.at[z], peer)
    spread(3, 8)
    for i in range(1, NZ):
        slot = lax.rem(z + i, NZ)
        landed(z_in.at[slot], z_recv.at[slot])
    y_in[y] = jnp.sum(z_in[...], axis=0)
    for peer in y_peers:
        push(y_in.at[y], y_in.at[y], y_recv.at[y], peer)
    spread(8, 12)
    for i in range(1, NY):
        slot = lax.rem(y + i, NY)
        landed(y_in.at[slot], y_recv.at[slot])
    final[core] = jnp.sum(y_in[...], axis=0) * (1.0 / math.sqrt(NX * 4 * count * ROWS))
    push(final.at[core], final.at[core], c_recv.at[1], other_core)
    landed(final.at[1 - core], c_recv.at[1])
    for half in range(2):
        for j in range(6):
            cols = slice((half * 6 + j) * 128, (half * 6 + j + 1) * 128)
            dw_ref[:, cols] = final[half, j * KW : (j + 1) * KW, :]
    for copy in started:
        copy.wait_send()


def run(queries, keys, values, features_fine, rc_state, conv_weight):
    vmem, hbm = pl.BlockSpec(memory_space=pltpu.VMEM), pl.BlockSpec(memory_space=pltpu.HBM)
    dma = pltpu.SemaphoreType.DMA
    n_sends = sum(len(s) for s in block_sends().values()) + 3 + 2 + 1 + 3 + 7 + 7 + 1
    return pl.pallas_call(
        kernel,
        name="attend_and_convolve",
        out_shape=(jax.ShapeDtypeStruct((2 * ROWS, D), BF16), jax.ShapeDtypeStruct((KW, D), F32)),
        in_specs=[hbm] * 5 + [vmem],
        out_specs=(vmem, vmem),
        scratch_shapes=[
            pltpu.VMEM((NY, NA, ROWS, DK), BF16),
            pltpu.VMEM((NY, NA, DV, 128), BF16),
            pltpu.VMEM((ROWS, D), BF16),
            pltpu.VMEM((HEADS, ROWS, DK), BF16),
            pltpu.VMEM((DK, NA * ROWS), BF16),
            pltpu.VMEM((NA * ROWS, 256), BF16),
            pltpu.VMEM((HEADS, ROWS, 128), F32),
            pltpu.VMEM((HEADS, ROWS, 256), F32),
            pltpu.VMEM((2 * ROWS, D), BF16),
            pltpu.VMEM((D // 128, 2 * ROWS, 128), F32),
            pltpu.VMEM((ROWS, D), F32),
            pltpu.VMEM((ROWS + 16, D), F32),
            pltpu.VMEM((ROWS + 16, D), F32),
            pltpu.VMEM((ROWS + 16, D), F32),
            pltpu.VMEM((2, 2, D), F32),
            pltpu.VMEM((2, 2, D), F32),
            pltpu.VMEM((2, 1, D), F32),
            pltpu.VMEM((2, 1, D), F32),
            pltpu.VMEM((2, 32, 128), F32),
            pltpu.VMEM((32, 128), F32),
            pltpu.VMEM((NX, 32, 128), F32),
            pltpu.VMEM((NZ, 32, 128), F32),
            pltpu.VMEM((NY, 32, 128), F32),
            pltpu.VMEM((2, 32, 128), F32),
            dma((11,)),
            dma((n_sends,)),
            dma((NY, NA)),
            dma((NY, NA)),
            dma,
            dma((2,)),
            dma((2,)),
            dma((2,)),
            dma((NX,)),
            dma((NZ,)),
            dma((NY,)),
        ],
        compiler_params=pltpu.CompilerParams(
            collective_id=0, has_side_effects=True, vmem_limit_bytes=40 * 2**20
        ),
    )(queries, keys, values, features_fine, rc_state, conv_weight)


def body(queries, keys, values, features_fine, rc_state, conv_weight):
    d_fine, d_weight = run(
        queries[0], keys[0], jnp.swapaxes(values[0], 0, 1), features_fine[0], rc_state[0], conv_weight
    )
    return d_fine[None], d_weight


def solution(mesh):
    split = P("dp", "ctx", None)
    return jax.shard_map(
        body, mesh=mesh, in_specs=(split,) * 5 + (P(),), out_specs=(split, P()), check_vma=False
    )
```

time: 198 us -> 113 us (0.57)
  blocking collectives: 105 us -> 0 us
  Pallas kernels: 86.3 us -> 105 us
  local copies, waits for them, and re-layouts: 4.88 us -> 6.93 us
    psum x1 -> x0, blocking collectives: 105 us -> none  [body(): summed = lax.psum(partial, ('dp', 'ctx'))]
    pallas_call x1, Pallas kernels: 86.3 us -> 105 us  [run(): pl.pallas_call(kernel, name='attend_and_convolve', out_shape=(jax.ShapeDt...]
    unnamed x12 -> x14, local copies, waits for them, and re-layouts: 4.88 us -> 6.93 us
where the time goes in v2:
time: 113 us
  Pallas kernels  105 us (93%)
  local copies, waits for them, and re-layouts  6.93 us (6%)
    pallas_call x1, Pallas kernels, run(): pl.pallas_call(kernel, name='attend_and_convolve', out_shape=(jax.ShapeDt...  105 us
    unnamed x14, local copies, waits for them, and re-layouts  6.93 us

profile of v2, /device:TPU:1, one launch (start us, length us, event | category | flops | bytes accessed | tf_op | source)
XLA Modules:
  0.0 112.7 jit_solution(6734787906336203920)
XLA Ops:
  0.6 0.0 copy-start
  0.6 1.1 copy-done
  1.8 0.0 copy-start.1
  1.8 1.0 copy-done.1
  2.8 0.0 copy-start.2
  2.8 0.9 copy-done.2
  3.7 0.0 copy-start.3
  3.7 0.8 copy-done.3
  4.5 0.0 copy-start.4
  4.5 0.8 copy-done.4
  5.3 0.0 copy-start.5
  5.3 0.8 copy-done.5
  6.1 105.1 %attend_and_convolve.1 = (bf16[256,1536]{1,0:T(8,128)(2,1)S(1)}, f32[5,1536]{1,0:T(8,128)S(1)}) custom-call(bf16[128,1024]{1,0:T(8,128)(2,1)S(1)} %bitcast.11, bf16[128,128]{1,0:T(8,128)(2,1)S(1)} %bitcast.13, bf16[192,128]{1,0:T(8,128)(2,1)S(1)} %bitcast.12, bf16[256,1536]{1,0:T(8,128)(2,1)S(1)} %bitcast.8, bf16[128,1536]{1,0:T(8,128)(2,1)S(1)} %bitcast.10, ...), custom_call_target="tpu_custom_call" | custom-call | tf_op jit(solution)/shard_map/attend_and_convolve/pallas_call | solution.py:324
  111.2 0.9 copy.10
  112.1 0.6 copy.11
Async XLA Ops:
  0.6 1.1 %copy-start = (bf16[1,256,1536]{2,1,0:T(8,128)(2,1)S(1)}, bf16[1,256,1536]{2,1,0:T(8,128)(2,1)}, u32[]{:S(2)}) copy-start(bf16[1,256,1536]{2,1,0:T(8,128)(2,1)} %param.9) | copy-start | bytes 2359300
  1.8 1.0 copy-start.1
  2.8 0.9 copy-start.2
  3.7 0.8 copy-start.3
  4.5 0.8 copy-start.4
  5.3 0.8 copy-start.5

commit v3 on v2

--- a/solution.py
+++ b/solution.py
@@ -14,6 +14,9 @@
 ROWS = 128
 D = HEADS * DV
 KW = 5
+KVROWS = DK + DV
+KPART = 128
+PIECES = 4
 NA, NY = 4, 8
 NX, NZ = 4, 8
 MESH = pl.DeviceIdType.MESH
@@ -23,65 +26,59 @@
 
 def block_sends():
     sends = {}
-    for da in range(NA):
-        cw = 4 - da % 2
+    for za in range(NA):
+        cw = 4 - za % 2
         for dy in range(NY):
             behind = (NY - dy) % NY
             v, k = [], []
             if dy == 0:
-                if da == 0:
-                    v += [("a+", ("V", 3, 0)), ("a-", ("V", 1, 0)), ("a2", ("V", 2, 0))]
-                v += [("y+", ("V", da, 7)), ("y-", ("V", da, 1))]
+                if za == 0:
+                    v += [("near", ("V", 1, 0)), ("far", ("V", 2, 0))]
+                if za == 2:
+                    v.append(("near", ("V", 3, 0)))
+                v += [("y+", ("V", za, 7)), ("y-", ("V", za, 1))]
             elif behind <= cw:
                 if behind < cw:
-                    v.append(("y+", ("V", da, dy - 1)))
+                    v.append(("y+", ("V", za, dy - 1)))
             elif dy < 7 - cw:
-                v.append(("y-", ("V", da, dy + 1)))
-            sends[("V", da, dy)] = v
-            if da == 0:
+                v.append(("y-", ("V", za, dy + 1)))
+            sends[("V", za, dy)] = v
+            if za == 0:
                 if dy == 0:
                     k += [("y+", ("K", 0, 7)), ("y-", ("K", 0, 1))]
                 elif behind < 4:
                     k.append(("y+", ("K", 0, dy - 1)))
                 elif dy < 3:
                     k.append(("y-", ("K", 0, dy + 1)))
-                k += [("a+", ("K", 3, dy)), ("a-", ("K", 1, dy))]
-            elif da == 3 and dy % 2 == 0:
-                k.append(("a+", ("K", 2, dy)))
-            elif da == 1 and dy % 2 == 1:
-                k.append(("a-", ("K", 2, dy)))
-            sends[("K", da, dy)] = k
+                k += [("near", ("K", 1, dy)), ("far", ("K", 2, dy))]
+            elif za == 2:
+                k.append(("near", ("K", 3, dy)))
+            sends[("K", za, dy)] = k
     return sends
 
 
 def arrival_order(sends):
-    free = {"y+": 0.0, "y-": 0.0, "a+": 0.0, "a-": 0.0}
-    cost = {"V": 1.06, "K": 0.71}
-    queue = [(0.0, 0, ("K", 0, 0)), (0.0, 1, ("V", 0, 0))]
+    free = {"y+": 0.0, "y-": 0.0, "near": 0.0, "far": 0.0}
+    slow = {"y+": 1.5, "y-": 1.5, "near": 2.0, "far": 4.0}
+    cost = {"V": (KVROWS - KPART) * 0.0055, "K": KPART * 0.0055}
+    queue = [(0.0, 0, ("V", 0, 0)), (0.0, 1, ("K", 0, 0))]
     order, n = [], 2
     while queue:
         now, _, key = heapq.heappop(queue)
         order.append(key)
         for link, child in sends[key]:
-            if link == "a2":
-                end = max(now, free["a+"], free["a-"]) + 2 * cost[key[0]]
-                free["a+"] = free["a-"] = end
-                late = 3.6
-            else:
-                along_y = link[0] == "y"
-                end = max(now, free[link]) + cost[key[0]] * (1 if along_y else 2)
-                free[link] = end
-                late = 1.8 if along_y else 2.4
-            heapq.heappush(queue, (end + late, n, child))
+            end = max(now, free[link]) + cost[key[0]] * slow[link]
+            free[link] = end
+            heapq.heappush(queue, (end + (1.8 if link[0] == "y" else 2.4), n, child))
             n += 1
     return order
 
 
 def kernel(
     q_ref, k_ref, v_ref, ff_ref, rc_ref, w_ref, df_ref, dw_ref,
-    kbuf, vbuf, rcin, qs, kx, vx, top, acc, fine, wide, base, ev, od, grd, halo_out, halo_in, edge_out, edge_in,
+    kv, relay, rcin, qs, kx, vx, top, acc, fine, wide, base, ev, od, grd, halo_out, halo_in, edge_out, edge_in,
     part, core_in, x_in, z_in, y_in, final,
-    local, send_sem, k_sem, v_sem, m_recv, h_recv, e_recv, c_recv, x_recv, z_recv, y_recv,
+    local, send_sem, k_sem, v_sem, m_sem, h_recv, e_recv, c_recv, x_recv, z_recv, y_recv,
 ):
     dp, ctx = lax.axis_index("dp"), lax.axis_index("ctx")
     a, y = ctx // NY, lax.rem(ctx, NY)
@@ -93,10 +90,10 @@
         return (dp, lax.rem(a_new, NA) * NY + lax.rem(y_new, NY))
 
     right, left = (dp, lax.rem(ctx + 1, count)), (dp, lax.rem(ctx + count - 1, count))
-    mirror = (dp, count - 1 - ctx)
-    peers = {
-        "y+": at(a, y + 1), "y-": at(a, y + NY - 1), "a+": at(a + 1, y), "a-": at(a + NA - 1, y), "a2": at(a + 2, y),
-    }
+    near, far = a + 1 - 2 * lax.rem(a, 2), NA - 1 - a
+    rows_of_a = (a, near, far, NA - 1 - near)
+    y_mirror = (dp, a * NY + NY - 1 - y)
+    peers = {"y+": at(a, y + 1), "y-": at(a, y + NY - 1), "near": at(near, y), "far": at(far, y)}
     other_core = (dp + 1 - 2 * core, ctx)
     x_peers = [(lax.rem(x + i, NX) * 4 + zlo * 2 + core, ctx) for i in range(1, NX)]
     z_peers = []
@@ -105,12 +102,12 @@
         z_peers.append((x * 4 + lax.rem(z_new, 2) * 2 + core, z_new // 2 * NY + y))
     y_peers = [at(a, y + i) for i in range(1, NY)]
     barrier = pltpu.get_barrier_semaphore()
-    greeted = [right, left, mirror, other_core] + x_peers + z_peers + y_peers
+    greeted = [right, left, y_mirror, other_core] + x_peers + z_peers + y_peers
     for peer in greeted:
         pl.semaphore_signal(barrier, inc=1, device_id=peer, device_id_type=MESH)
 
-    own_k = pltpu.make_async_copy(k_ref, kbuf.at[y, a], local.at[0])
-    own_v = pltpu.make_async_copy(v_ref, vbuf.at[y, a, pl.ds(0, DV)], local.at[1])
+    own_k = pltpu.make_async_copy(k_ref, kv.at[y, a, pl.ds(0, DK)], local.at[0])
+    own_v = pltpu.make_async_copy(v_ref, kv.at[y, a, pl.ds(DK, DV)], local.at[1])
     own_f = pltpu.make_async_copy(ff_ref, fine, local.at[2])
     own_q = [
         pltpu.make_async_copy(q_ref.at[:, pl.ds(h * DK, DK)], qs.at[h], local.at[3 + h]) for h in range(HEADS)
@@ -134,15 +131,34 @@
     order = arrival_order(sends)
 
     def event(key):
-        o_a, o_y = lax.rem(a + key[1], NA), lax.rem(y + key[2], NY)
+        o_a, o_y = rows_of_a[key[1]], lax.rem(y + key[2], NY)
         if key[0] == "K":
-            ref, sem = kbuf.at[o_y, o_a], k_sem.at[o_y, o_a]
+            ref, sem = kv.at[o_y, o_a, pl.ds(0, KPART)], k_sem.at[o_y, o_a]
         else:
-            ref, sem = vbuf.at[o_y, o_a, pl.ds(0, DV)], v_sem.at[o_y, o_a]
+            ref, sem = kv.at[o_y, o_a, pl.ds(KPART, KVROWS - KPART)], v_sem.at[o_y, o_a]
         if key[1:] != (0, 0):
             landed(ref, sem)
         for link, _ in sends[key]:
             push(ref, ref, sem, peers[link])
+
+    step = ROWS // 2 // PIECES
+
+    def lanes(i):
+        one, two = pl.ds(i * step, step), pl.ds(ROWS // 2 + i * step, step)
+        return ((one, 0, y_mirror, peers["far"]), (two, 1, peers["far"], y_mirror))
+
+    def reflect(i):
+        for rows, way, peer, _ in lanes(i):
+            push(rc_ref.at[rows], relay.at[rows], m_sem.at[way, i], peer)
+
+    def reflect_on(i):
+        for rows, way, _, peer in lanes(i):
+            landed(relay.at[rows], m_sem.at[way, i])
+            push(relay.at[rows], rcin.at[rows], m_sem.at[2 + way, i], peer)
+
+    def reflected(i):
+        for rows, way, _, _ in lanes(i):
+            landed(rcin.at[rows], m_sem.at[2 + way, i])
 
     def prepare():
         def heads(h, _):
@@ -157,27 +173,34 @@
         o_y = lax.rem(y + dy, NY)
         for i in range(NA):
             rows = slice(i * ROWS, (i + 1) * ROWS)
-            kx[:, rows] = kbuf[o_y, i].T
-            vx[rows, 0:128] = vbuf[o_y, i, 0:128, :].T
-            vx[rows, 128:192] = vbuf[o_y, i, 128:192, :].T
+            kx[:, rows] = kv[o_y, i, 0:DK, :].T
+            vx[rows, 0:128] = kv[o_y, i, DK : DK + 128, :].T
+            vx[rows, 128:192] = kv[o_y, i, DK + 128 : DK + DV, :].T
 
     factor = DK ** (-0.5) * math.log2(math.e)
 
-    def attend(low, high):
-        def head(h, _):
-            s = jnp.dot(qs[h], kx[...], preferred_element_type=F32)
-            old = top[h]
-            new = jnp.maximum(old, jnp.max(s, axis=1, keepdims=True))
-            p = jnp.exp2((s - new[:, :1]) * factor).astype(BF16)
-            fade = jnp.exp2((old - new) * factor)
-            fade = jnp.concatenate([fade, fade], axis=1)
-            acc[h] = acc[h] * fade + jnp.dot(p, vx[...], preferred_element_type=F32)
-            top[h] = new
+    def attend():
+        s = jnp.dot(qs[...].reshape(HEADS * ROWS, DK), kx[...], preferred_element_type=F32)
+        old = top[...].reshape(HEADS * ROWS, 128)
+        new = jnp.maximum(old, jnp.max(s, axis=1, keepdims=True))
+        p = jnp.exp2((s - new[:, :1]) * factor).astype(BF16)
+        fade = jnp.exp2((old - new) * factor)
+        fade = jnp.concatenate([fade, fade], axis=1)
+        total = acc[...].reshape(HEADS * ROWS, 256) * fade + jnp.dot(p, vx[...], preferred_element_type=F32)
+        acc[...] = total.reshape(HEADS, ROWS, 256)
+        top[...] = new.reshape(HEADS, ROWS, 128)
+
+    def widen():
+        def chunk(i, _):
+            cols = pl.ds(pl.multiple_of(i * 128, 128), 128)
+            wide[i] = fine[:, cols].astype(F32)
+            ev[8:136, cols] = wide[i, pl.ds(0, ROWS, stride=2), :]
+            od[8:136, cols] = wide[i, pl.ds(1, ROWS, stride=2), :]
             return 0
 
-        lax.fori_loop(low, high, head, 0)
-
-    def convolve():
+        lax.fori_loop(0, D // 128, chunk, 0)
+
+    def take_halo():
         landed(halo_in.at[0], h_recv.at[0])
         landed(halo_in.at[1], h_recv.at[1])
         inner_left = jnp.where(ctx > 0, 1.0, 0.0)
@@ -186,11 +209,9 @@
         od[7:8, :] = halo_in[0, 1:2, :] * inner_left
         ev[136:137, :] = halo_in[1, 0:1, :] * inner_right
 
+    def convolve(low, high):
         def chunk(i, _):
             cols = pl.ds(pl.multiple_of(i * 128, 128), 128)
-            wide[i] = fine[:, cols].astype(F32)
-            ev[8:136, cols] = wide[i, pl.ds(0, ROWS, stride=2), :]
-            od[8:136, cols] = wide[i, pl.ds(1, ROWS, stride=2), :]
             w = w_ref[:, cols]
             base[:, cols] = (
                 w[0:1] * ev[7:135, cols]
@@ -201,7 +222,7 @@
             )
             return 0
 
-        lax.fori_loop(0, D // 128, chunk, 0)
+        lax.fori_loop(low, high, chunk, 0)
 
     own_f.wait()
     halo_out[0] = fine[2 * ROWS - 16 : 2 * ROWS, :].astype(F32)[14:16]
@@ -211,33 +232,36 @@
     pl.semaphore_wait(barrier, len(greeted))
 
     ready, done = [], {}
+    out, back = 0, 0
     for n, key in enumerate(order):
         event(key)
+        if out < PIECES and n >= 1 + out * 8:
+            reflect(out)
+            out += 1
         if n == 1:
             push(halo_out.at[0], halo_in.at[0], h_recv.at[0], right)
             push(halo_out.at[1], halo_in.at[1], h_recv.at[1], left)
-            push(rc_ref, rcin, m_recv, mirror)
             for copy in own_q:
                 copy.wait()
             prepare()
-        if n == 9:
-            convolve()
+            widen()
+        if back < out and n >= 20 + back * 12:
+            reflect_on(back)
+            back += 1
+        if n == 7:
+            take_halo()
+        if n in (8, 10, 12, 14):
+            convolve((n - 8) // 2 * 3, (n - 8) // 2 * 3 + 3)
         done[key[2]] = done.get(key[2], 0) + 1
         if done[key[2]] == 2 * NA:
-            ready += [(key[2], h) for h in range(0, HEADS, 2)]
-        if n < len(order) - 1 and ready:
-            dy, h = ready.pop(0)
-            if h == 0:
-                gather_keys(dy)
-            attend(h, h + 2)
-    while ready:
-        dy, h = ready[0]
-        if h == 0:
-            gather_keys(dy)
-        attend(h, HEADS)
-        ready = [r for r in ready if r[0] != dy]
-
-    landed(rcin, m_recv)
+            ready.append(key[2])
+        if ready:
+            gather_keys(ready.pop(0))
+            attend()
+    for i in range(back, PIECES):
+        reflect_on(i)
+    for i in range(PIECES):
+        reflected(i)
     row = lax.broadcasted_iota(jnp.int32, (ROWS, ROWS), 0)
     col = lax.broadcasted_iota(jnp.int32, (ROWS, ROWS), 1)
     turn = jnp.where(row + col == ROWS - 1, 1.0, 0.0).astype(BF16)
@@ -320,7 +344,7 @@
 def run(queries, keys, values, features_fine, rc_state, conv_weight):
     vmem, hbm = pl.BlockSpec(memory_space=pltpu.VMEM), pl.BlockSpec(memory_space=pltpu.HBM)
     dma = pltpu.SemaphoreType.DMA
-    n_sends = sum(len(s) for s in block_sends().values()) + 3 + 2 + 1 + 3 + 7 + 7 + 1
+    n_sends = sum(len(s) for s in block_sends().values()) + 4 * PIECES + 2 + 2 + 1 + 3 + 7 + 7 + 1
     return pl.pallas_call(
         kernel,
         name="attend_and_convolve",
@@ -328,8 +352,8 @@
         in_specs=[hbm] * 5 + [vmem],
         out_specs=(vmem, vmem),
         scratch_shapes=[
-            pltpu.VMEM((NY, NA, ROWS, DK), BF16),
-            pltpu.VMEM((NY, NA, DV, 128), BF16),
+            pltpu.VMEM((NY, NA, KVROWS, 128), BF16),
+            pltpu.VMEM((ROWS, D), BF16),
             pltpu.VMEM((ROWS, D), BF16),
             pltpu.VMEM((HEADS, ROWS, DK), BF16),
             pltpu.VMEM((DK, NA * ROWS), BF16),
@@ -356,7 +380,7 @@
             dma((n_sends,)),
             dma((NY, NA)),
             dma((NY, NA)),
-            dma,
+            dma((4, PIECES)),
             dma((2,)),
             dma((2,)),
             dma((2,)),
@@ -365,7 +389,7 @@
             dma((NY,)),
         ],
         compiler_params=pltpu.CompilerParams(
-            collective_id=0, has_side_effects=True, vmem_limit_bytes=40 * 2**20
+            collective_id=0, has_side_effects=True, vmem_limit_bytes=62 * 2**20
         ),
     )(queries, keys, values, features_fine, rc_state, conv_weight)
 

time: 113 us -> 84.3 us (0.75)
  Pallas kernels: 105 us -> 80.7 us
  local copies, waits for them, and re-layouts: 6.93 us -> 2.7 us
    pallas_call x1, Pallas kernels: 105 us -> 80.7 us  [run(): pl.pallas_call(kernel, name='attend_and_convolve', out_shape=(jax.ShapeDt...]
    unnamed x14 -> x4, local copies, waits for them, and re-layouts: 6.93 us -> 2.7 us
where the time goes in v3:
time: 84.3 us; the launch traced here: 84.1 us
  Pallas kernels  80.7 us (96%)
  local copies, waits for them, and re-layouts  2.7 us (3%)
    pallas_call x1, Pallas kernels, run(): pl.pallas_call(kernel, name='attend_and_convolve', out_shape=(jax.ShapeDt...  80.7 us
    unnamed x4, local copies, waits for them, and re-layouts  2.7 us

profile of v3, /device:TPU:1, one launch (start us, length us, event | category | flops | bytes accessed | tf_op | source)
XLA Modules:
  0.0 84.1 jit_solution(17618543416376442192)
XLA Ops:
  0.6 80.7 %attend_and_convolve.1 = (bf16[256,1536]{1,0:T(8,128)(2,1)}, f32[5,1536]{1,0:T(8,128)}) custom-call(bf16[128,1024]{1,0:T(8,128)(2,1)} %bitcast.11, bf16[128,128]{1,0:T(8,128)(2,1)} %bitcast.13, bf16[192,128]{1,0:T(8,128)(2,1)} %bitcast.12, bf16[256,1536]{1,0:T(8,128)(2,1)} %bitcast.8, bf16[128,1536]{1,0:T(8,128)(2,1)} %bitcast.10, f32[5,1536]{1,0:T(8,128)} %w_ref.1), custom_call_target="tpu_custom_call" | custom-call | tf_op jit(solution)/shard_map/attend_and_convolve/pallas_call | solution.py:348
  81.4 0.0 copy-start
  81.4 2.1 %copy.10 = bf16[1,256,1536]{2,1,0:T(8,128)(2,1)} copy(bf16[1,256,1536]{2,1,0:T(8,128)(2,1)} %bitcast.9) | data formatting | bytes 1572864
  83.5 0.0 copy-done
  83.5 0.6 copy.11
Async XLA Ops:
  81.4 2.1 %copy-start = (f32[5,1536]{1,0:T(8,128)S(1)}, f32[5,1536]{1,0:T(8,128)}, u32[]{:S(2)}) copy-start(f32[5,1536]{1,0:T(8,128)} %get-tuple-element.9) | copy-start | bytes 92164

commit v4 on v3

--- a/solution.py
+++ b/solution.py
@@ -15,7 +15,7 @@
 D = HEADS * DV
 KW = 5
 KVROWS = DK + DV
-KPART = 128
+KPART = 112
 PIECES = 4
 NA, NY = 4, 8
 NX, NZ = 4, 8
@@ -75,10 +75,10 @@
 
 
 def kernel(
-    q_ref, k_ref, v_ref, ff_ref, rc_ref, w_ref, df_ref, dw_ref,
-    kv, relay, rcin, qs, kx, vx, top, acc, fine, wide, base, ev, od, grd, halo_out, halo_in, edge_out, edge_in,
-    part, core_in, x_in, z_in, y_in, final,
-    local, send_sem, k_sem, v_sem, m_sem, h_recv, e_recv, c_recv, x_recv, z_recv, y_recv,
+    q_ref, k_ref, v_ref, ff_ref, rc_ref, cw_ref, df_ref, dw_ref,
+    w_ref, kv, relay, rcin, qs, kx, vx, top, acc, fine, wide, base, ev, od, grd, halo_out, halo_in, edge_out, edge_in,
+    part, e_in, z_in, y_in, final,
+    local, send_sem, k_sem, v_sem, m_sem, h_recv, e_recv, s_send, s_recv, z_recv, y_recv, f_recv,
 ):
     dp, ctx = lax.axis_index("dp"), lax.axis_index("ctx")
     a, y = ctx // NY, lax.rem(ctx, NY)
@@ -95,14 +95,18 @@
     y_mirror = (dp, a * NY + NY - 1 - y)
     peers = {"y+": at(a, y + 1), "y-": at(a, y + NY - 1), "near": at(near, y), "far": at(far, y)}
     other_core = (dp + 1 - 2 * core, ctx)
-    x_peers = [(lax.rem(x + i, NX) * 4 + zlo * 2 + core, ctx) for i in range(1, NX)]
+    e = x * 2 + core
+    e_peers = []
+    for i in range(1, 8):
+        e_new = lax.rem(e + i, 8)
+        e_peers.append((e_new // 2 * 4 + zlo * 2 + lax.rem(e_new, 2), ctx))
     z_peers = []
     for i in range(1, NZ):
         z_new = lax.rem(z + i, NZ)
         z_peers.append((x * 4 + lax.rem(z_new, 2) * 2 + core, z_new // 2 * NY + y))
     y_peers = [at(a, y + i) for i in range(1, NY)]
     barrier = pltpu.get_barrier_semaphore()
-    greeted = [right, left, y_mirror, other_core] + x_peers + z_peers + y_peers
+    greeted = [right, left, y_mirror] + e_peers + z_peers + y_peers
     for peer in greeted:
         pl.semaphore_signal(barrier, inc=1, device_id=peer, device_id_type=MESH)
 
@@ -112,7 +116,8 @@
     own_q = [
         pltpu.make_async_copy(q_ref.at[:, pl.ds(h * DK, DK)], qs.at[h], local.at[3 + h]) for h in range(HEADS)
     ]
-    for copy in [own_f, own_k, own_v] + own_q:
+    own_w = pltpu.make_async_copy(cw_ref, w_ref, local.at[3 + HEADS])
+    for copy in [own_f, own_k, own_v] + own_q + [own_w]:
         copy.start()
 
     started = []
@@ -241,7 +246,7 @@
         if n == 1:
             push(halo_out.at[0], halo_in.at[0], h_recv.at[0], right)
             push(halo_out.at[1], halo_in.at[1], h_recv.at[1], left)
-            for copy in own_q:
+            for copy in own_q + [own_w]:
                 copy.wait()
             prepare()
             widen()
@@ -255,9 +260,12 @@
         done[key[2]] = done.get(key[2], 0) + 1
         if done[key[2]] == 2 * NA:
             ready.append(key[2])
-        if ready:
+        if ready and (n > len(order) - 2 or (done[key[2]] != 2 * NA)):
             gather_keys(ready.pop(0))
             attend()
+    while ready:
+        gather_keys(ready.pop(0))
+        attend()
     for i in range(back, PIECES):
         reflect_on(i)
     for i in range(PIECES):
@@ -266,31 +274,34 @@
     col = lax.broadcasted_iota(jnp.int32, (ROWS, ROWS), 1)
     turn = jnp.where(row + col == ROWS - 1, 1.0, 0.0).astype(BF16)
 
-    def finish(j, _):
-        cols = pl.ds(pl.multiple_of(j * 2 * DV, 128), 2 * DV)
+    part[60:64, :] = jnp.zeros((4, 128), F32)
+    shared, given = [], 0
+    for j in range(HEADS // 2):
+        cols = slice(j * 2 * DV, (j + 1) * 2 * DV)
         one, two = acc[2 * j], acc[2 * j + 1]
         attended = jnp.concatenate(
             [one[:, :DV] / one[:, DV : DV + 1], two[:, :DV] / two[:, DV : DV + 1]], axis=1
         )
         grd[8:136, cols] = base[:, cols] + attended - jnp.dot(turn, rcin[:, cols], preferred_element_type=F32)
-        return 0
-
-    lax.fori_loop(0, HEADS // 2, finish, 0)
+        for i in range(3 * j, 3 * j + 3):
+            cols = slice(i * 128, (i + 1) * 128)
+            g = grd[8:136, cols]
+            taps = (ev[7:135, cols], od[7:135, cols], ev[8:136, cols], od[8:136, cols], ev[9:137, cols])
+            part[i * KW : (i + 1) * KW, :] = jnp.concatenate(
+                [jnp.sum(g * tap, axis=0, keepdims=True) for tap in taps], axis=0
+            )
+        while given < 8 and (8 * given + 8 <= 15 * (j + 1) or j == 3):
+            copy = pltpu.make_async_remote_copy(
+                part.at[pl.ds(8 * given, 8)], e_in.at[e], s_send.at[given], s_recv.at[e],
+                device_id=(given // 2 * 4 + zlo * 2 + given % 2, ctx), device_id_type=MESH,
+            )
+            pl.when(e != given)(copy.start)
+            shared.append(copy)
+            given += 1
     edge_out[0] = grd[135:136, :]
     edge_out[1] = grd[8:9, :]
     push(edge_out.at[0], edge_in.at[0], e_recv.at[0], right)
     push(edge_out.at[1], edge_in.at[1], e_recv.at[1], left)
-
-    part[:, 30:32, :] = jnp.zeros((2, 2, 128), F32)
-    for half in range(2):
-        for j in range(6):
-            cols = slice((half * 6 + j) * 128, (half * 6 + j + 1) * 128)
-            g = grd[8:136, cols]
-            taps = (ev[7:135, cols], od[7:135, cols], ev[8:136, cols], od[8:136, cols], ev[9:137, cols])
-            part[half, j * KW : (j + 1) * KW, :] = jnp.concatenate(
-                [jnp.sum(g * tap, axis=0, keepdims=True) for tap in taps], axis=0
-            )
-    push(part.at[1 - core], core_in, c_recv.at[0], other_core)
 
     def spread(low, high):
         def chunk(i, _):
@@ -304,39 +315,39 @@
 
         lax.fori_loop(low, high, chunk, 0)
 
-    landed(core_in, c_recv.at[0])
-    x_in[x] = part[core] + core_in[...]
-    for i, peer in enumerate(x_peers):
-        push(x_in.at[x], x_in.at[x], x_recv.at[x], peer)
+    e_in[e] = part[pl.ds(pl.multiple_of(8 * e, 8), 8), :]
+    for i in range(1, 8):
+        slot = lax.rem(e + i, 8)
+        landed(e_in.at[slot], s_recv.at[slot])
+    z_in[z] = jnp.sum(e_in[...], axis=0)
+    for peer in z_peers:
+        push(z_in.at[z], z_in.at[z], z_recv.at[z], peer)
     landed(edge_in.at[0], e_recv.at[0])
     landed(edge_in.at[1], e_recv.at[1])
     grd[7:8, :] = edge_in[0] * jnp.where(ctx > 0, 1.0, 0.0)
     grd[136:137, :] = edge_in[1] * jnp.where(ctx < count - 1, 1.0, 0.0)
-    spread(0, 3)
-    for i in range(1, NX):
-        slot = lax.rem(x + i, NX)
-        landed(x_in.at[slot], x_recv.at[slot])
-    z_in[z] = jnp.sum(x_in[...], axis=0)
-    for peer in z_peers:
-        push(z_in.at[z], z_in.at[z], z_recv.at[z], peer)
-    spread(3, 8)
+    spread(0, 6)
     for i in range(1, NZ):
         slot = lax.rem(z + i, NZ)
         landed(z_in.at[slot], z_recv.at[slot])
     y_in[y] = jnp.sum(z_in[...], axis=0)
     for peer in y_peers:
         push(y_in.at[y], y_in.at[y], y_recv.at[y], peer)
-    spread(8, 12)
+    spread(6, 12)
     for i in range(1, NY):
         slot = lax.rem(y + i, NY)
         landed(y_in.at[slot], y_recv.at[slot])
-    final[core] = jnp.sum(y_in[...], axis=0) * (1.0 / math.sqrt(NX * 4 * count * ROWS))
-    push(final.at[core], final.at[core], c_recv.at[1], other_core)
-    landed(final.at[1 - core], c_recv.at[1])
-    for half in range(2):
-        for j in range(6):
-            cols = slice((half * 6 + j) * 128, (half * 6 + j + 1) * 128)
-            dw_ref[:, cols] = final[half, j * KW : (j + 1) * KW, :]
+    final[pl.ds(pl.multiple_of(8 * e, 8), 8), :] = jnp.sum(y_in[...], axis=0) * (1.0 / math.sqrt(NX * 4 * count * ROWS))
+    mine = final.at[pl.ds(pl.multiple_of(8 * e, 8), 8)]
+    for peer in e_peers:
+        push(mine, mine, f_recv.at[e], peer)
+    for i in range(1, 8):
+        slot = lax.rem(e + i, 8)
+        landed(final.at[pl.ds(pl.multiple_of(8 * slot, 8), 8)], f_recv.at[slot])
+    for i in range(D // 128):
+        dw_ref[:, i * 128 : (i + 1) * 128] = final[i * KW : (i + 1) * KW, :]
+    for i, copy in enumerate(shared):
+        pl.when(e != i)(copy.wait_send)
     for copy in started:
         copy.wait_send()
 
@@ -344,14 +355,15 @@
 def run(queries, keys, values, features_fine, rc_state, conv_weight):
     vmem, hbm = pl.BlockSpec(memory_space=pltpu.VMEM), pl.BlockSpec(memory_space=pltpu.HBM)
     dma = pltpu.SemaphoreType.DMA
-    n_sends = sum(len(s) for s in block_sends().values()) + 4 * PIECES + 2 + 2 + 1 + 3 + 7 + 7 + 1
+    n_sends = sum(len(s) for s in block_sends().values()) + 4 * PIECES + 2 + 2 + 7 + 7 + 7
     return pl.pallas_call(
         kernel,
         name="attend_and_convolve",
-        out_shape=(jax.ShapeDtypeStruct((2 * ROWS, D), BF16), jax.ShapeDtypeStruct((KW, D), F32)),
-        in_specs=[hbm] * 5 + [vmem],
+        out_shape=(pltpu.VMEM((2 * ROWS, D), BF16), pltpu.VMEM((KW, D), F32)),
+        in_specs=[hbm] * 6,
         out_specs=(vmem, vmem),
         scratch_shapes=[
+            pltpu.VMEM((KW, D), F32),
             pltpu.VMEM((NY, NA, KVROWS, 128), BF16),
             pltpu.VMEM((ROWS, D), BF16),
             pltpu.VMEM((ROWS, D), BF16),
@@ -370,23 +382,23 @@
             pltpu.VMEM((2, 2, D), F32),
             pltpu.VMEM((2, 1, D), F32),
             pltpu.VMEM((2, 1, D), F32),
-            pltpu.VMEM((2, 32, 128), F32),
-            pltpu.VMEM((32, 128), F32),
-            pltpu.VMEM((NX, 32, 128), F32),
-            pltpu.VMEM((NZ, 32, 128), F32),
-            pltpu.VMEM((NY, 32, 128), F32),
-            pltpu.VMEM((2, 32, 128), F32),
-            dma((11,)),
+            pltpu.VMEM((64, 128), F32),
+            pltpu.VMEM((8, 8, 128), F32),
+            pltpu.VMEM((NZ, 8, 128), F32),
+            pltpu.VMEM((NY, 8, 128), F32),
+            pltpu.VMEM((64, 128), F32),
+            dma((12,)),
             dma((n_sends,)),
             dma((NY, NA)),
             dma((NY, NA)),
             dma((4, PIECES)),
             dma((2,)),
             dma((2,)),
-            dma((2,)),
-            dma((NX,)),
+            dma((8,)),
+            dma((8,)),
             dma((NZ,)),
             dma((NY,)),
+            dma((8,)),
         ],
         compiler_params=pltpu.CompilerParams(
             collective_id=0, has_side_effects=True, vmem_limit_bytes=62 * 2**20

time: 84.3 us -> 78.4 us (0.930)
  Pallas kernels: 80.7 us -> 76.1 us
  local copies, waits for them, and re-layouts: 2.7 us -> 1.5 us
    pallas_call x1, Pallas kernels: 80.7 us -> 76.1 us  [run(): pl.pallas_call(kernel, name='attend_and_convolve', out_shape=(pltpu.VMEM(...]
    unnamed x4 -> x2, local copies, waits for them, and re-layouts: 2.7 us -> 1.5 us
where the time goes in v4:
time: 78.4 us; the launch traced here: 78.2 us
  Pallas kernels  76.1 us (97%)
  local copies, waits for them, and re-layouts  1.5 us (2%)
    pallas_call x1, Pallas kernels, run(): pl.pallas_call(kernel, name='attend_and_convolve', out_shape=(pltpu.VMEM(...  76.1 us

profile of v4, /device:TPU:1, one launch (start us, length us, event | category | flops | bytes accessed | tf_op | source)
XLA Modules:
  0.0 78.2 jit_solution(11388617637946596486)
XLA Ops:
  0.6 76.1 %attend_and_convolve.1 = (bf16[256,1536]{1,0:T(8,128)(2,1)S(1)}, f32[5,1536]{1,0:T(8,128)S(1)}) custom-call(bf16[128,1024]{1,0:T(8,128)(2,1)} %bitcast.11, bf16[128,128]{1,0:T(8,128)(2,1)} %bitcast.13, bf16[192,128]{1,0:T(8,128)(2,1)} %bitcast.12, bf16[256,1536]{1,0:T(8,128)(2,1)} %bitcast.9, bf16[128,1536]{1,0:T(8,128)(2,1)} %bitcast.10, f32[5,1536]{1,0:T(8,128)} %cw_ref.1), custom_call_target="tpu_custom_call" | custom-call | tf_op jit(solution)/shard_map/attend_and_convolve/pallas_call | solution.py:359
  76.7 0.9 %copy.10 = bf16[1,256,1536]{2,1,0:T(8,128)(2,1)} copy(bf16[1,256,1536]{2,1,0:T(8,128)(2,1)S(1)} %bitcast.8) | data formatting | bytes 1572864
  77.6 0.6 copy.11

commit v5 on v4

--- a/solution.py
+++ b/solution.py
@@ -117,7 +117,7 @@
         pltpu.make_async_copy(q_ref.at[:, pl.ds(h * DK, DK)], qs.at[h], local.at[3 + h]) for h in range(HEADS)
     ]
     own_w = pltpu.make_async_copy(cw_ref, w_ref, local.at[3 + HEADS])
-    for copy in [own_f, own_k, own_v] + own_q + [own_w]:
+    for copy in [own_k, own_v, own_f] + own_q + [own_w]:
         copy.start()
 
     started = []
@@ -229,9 +229,6 @@
 
         lax.fori_loop(low, high, chunk, 0)
 
-    own_f.wait()
-    halo_out[0] = fine[2 * ROWS - 16 : 2 * ROWS, :].astype(F32)[14:16]
-    halo_out[1] = fine[0:16, :].astype(F32)[0:2]
     own_k.wait()
     own_v.wait()
     pl.semaphore_wait(barrier, len(greeted))
@@ -244,13 +241,16 @@
             reflect(out)
             out += 1
         if n == 1:
+            own_f.wait()
+            halo_out[0] = fine[2 * ROWS - 16 : 2 * ROWS, :].astype(F32)[14:16]
+            halo_out[1] = fine[0:16, :].astype(F32)[0:2]
             push(halo_out.at[0], halo_in.at[0], h_recv.at[0], right)
             push(halo_out.at[1], halo_in.at[1], h_recv.at[1], left)
             for copy in own_q + [own_w]:
                 copy.wait()
             prepare()
             widen()
-        if back < out and n >= 20 + back * 12:
+        if back < out and n >= 26 + back * 11:
             reflect_on(back)
             back += 1
         if n == 7:

time: 78.4 us -> 78.6 us (level)
  no operation moved by 1% of the time
where the time goes in v5:
time: 78.6 us; the launch traced here: 78.4 us
  Pallas kernels  76.3 us (97%)
  local copies, waits for them, and re-layouts  1.5 us (2%)
    pallas_call x1, Pallas kernels, run(): pl.pallas_call(kernel, name='attend_and_convolve', out_shape=(pltpu.VMEM(...  76.3 us

profile of v5, /device:TPU:1, one launch (start us, length us, event | category | flops | bytes accessed | tf_op | source)
XLA Modules:
  0.0 78.4 jit_solution(4853453607189916353)
XLA Ops:
  0.6 76.3 %attend_and_convolve.1 = (bf16[256,1536]{1,0:T(8,128)(2,1)S(1)}, f32[5,1536]{1,0:T(8,128)S(1)}) custom-call(bf16[128,1024]{1,0:T(8,128)(2,1)} %bitcast.11, bf16[128,128]{1,0:T(8,128)(2,1)} %bitcast.13, bf16[192,128]{1,0:T(8,128)(2,1)} %bitcast.12, bf16[256,1536]{1,0:T(8,128)(2,1)} %bitcast.9, bf16[128,1536]{1,0:T(8,128)(2,1)} %bitcast.10, f32[5,1536]{1,0:T(8,128)} %cw_ref.1), custom_call_target="tpu_custom_call" | custom-call | tf_op jit(solution)/shard_map/attend_and_convolve/pallas_call | solution.py:359
  76.9 0.9 %copy.10 = bf16[1,256,1536]{2,1,0:T(8,128)(2,1)} copy(bf16[1,256,1536]{2,1,0:T(8,128)(2,1)S(1)} %bitcast.8) | data formatting | bytes 1572864
  77.8 0.6 copy.11
